TPU v7x, 32 devices: a whole 2x2x4 slice. The times are simulated.
32 devices in a mesh: row: 4 (over x, core), col: 8 (over z, y).
Axes of the slice: x: 2, y: 2, z: 4, core: 2. Of those that a mesh axis runs over, the one named last changes fastest.
Arguments:
- gradient: bfloat16 [6144, 24576], P('row', 'col'), may hold values from -60 to 60
Outputs:
- update: bfloat16 [6144, 24576], P('row', 'col')
All inputs are finite; a program needn't handle non-finite values.
Results may differ from a plain program's by a relative error of at most 0.001.
The roundings to bfloat16 on the way count: a program that leaves them out, or rounds other values in their place, can miss the bound.
Values may be sent and summed in bfloat16 or wider, within the bound.
A program may use at most 128 MiB of HBM per device.

v0:
```python
import jax
import jax.numpy as jnp
from jax import lax
from jax.sharding import PartitionSpec as P

M = 6144
BLOCK = 1536


damping = 0.001


def swapped(block, axis, apart):
    count = lax.axis_size(axis)
    route = []
    for low in range(count):
        high = low | 1 << apart
        if high != low and high < count:
            route += [(low, high), (high, low)]
    return lax.ppermute(block, axis, route)


def local(gradient):
    rows_dev, cols_dev = gradient.shape
    col_blocks = cols_dev // BLOCK
    share_count = BLOCK // rows_dev
    sections = share_count.bit_length() - 1
    row_count = lax.axis_size("row")
    row_index = lax.axis_index("row")
    row_blocks = M // BLOCK
    my_block = row_index // share_count
    offset = row_index % share_count * rows_dev
    slots = (jnp.arange(row_blocks) == my_block).astype(jnp.float32)
    band = gradient
    for bit in range(sections):
        partner = swapped(band, "row", bit)
        upper = row_index // 2**bit % 2 == 1
        band = jnp.where(
            upper, jnp.concatenate([partner, band], 0), jnp.concatenate([band, partner], 0)
        )
    grad_three = gradient.reshape(rows_dev, col_blocks, BLOCK)
    grad_wide = grad_three.astype(jnp.float32)
    grad_tiles = jnp.sum(grad_wide * grad_wide, axis=(0, 2))
    grad_slots = slots[:, None] * grad_tiles[None, :]
    grad_total = lax.psum(grad_slots, "row")
    left_part = lax.dot_general(
        gradient, band, (((1,), (1,)), ((), ())), preferred_element_type=jnp.float32
    )
    row_place = offset + lax.broadcasted_iota(jnp.int32, (rows_dev, 1), 0)
    left_rows = lax.psum(left_part, "col")
    diagonal = (lax.broadcasted_iota(jnp.int32, (rows_dev, BLOCK), 1) == row_place).astype(
        jnp.float32
    )
    left_rows = left_rows + damping * diagonal
    left_total = lax.psum(slots * jnp.sum(left_rows * left_rows), "row")
    left_scale = jnp.sqrt(jnp.sum(left_total * slots))
    left_root = ((5.0 * diagonal - left_rows / left_scale) * 0.25 * left_scale ** (-0.25)).astype(
        jnp.bfloat16
    )
    right_rows = BLOCK // row_count
    portion = grad_three
    right_share = lax.psum_scatter(
        jnp.einsum("rjc,rjd->cjd", portion, grad_three, preferred_element_type=jnp.float32),
        "row",
        scatter_dimension=0,
        tiled=True,
    )
    right_place = row_index * right_rows + lax.broadcasted_iota(
        jnp.int32, (right_rows, 1, BLOCK), 0
    )
    right_diagonal = (
        lax.broadcasted_iota(jnp.int32, (right_rows, 1, BLOCK), 2) == right_place
    ).astype(jnp.float32)
    right_share = right_share + damping * right_diagonal
    right_squares = jnp.sum(right_share * right_share, axis=(0, 2))
    right_total = lax.psum(right_squares, "row")
    right_scale = jnp.sqrt(right_total)[None, :, None]
    right_piece = (
        (5.0 * right_diagonal - right_share / right_scale) * 0.25 * right_scale ** (-0.25)
    ).astype(jnp.bfloat16)
    portion = grad_three
    projected = jnp.einsum(
        "rjc,cjd->rjd",
        portion,
        lax.all_gather(right_piece, "row", axis=0, tiled=True),
        preferred_element_type=jnp.float32,
    ).astype(jnp.bfloat16)
    projected_band = projected
    for bit in range(sections):
        partner_rows = swapped(projected_band, "row", bit)
        upper = row_index // 2**bit % 2 == 1
        projected_band = jnp.where(
            upper,
            jnp.concatenate([partner_rows, projected_band], 0),
            jnp.concatenate([projected_band, partner_rows], 0),
        )
    precond = jnp.einsum(
        "rk,kjd->rjd", left_root, projected_band, preferred_element_type=jnp.float32
    )
    pre_tiles = jnp.sum(precond * precond, axis=(0, 2))
    update_total = lax.psum(slots[:, None] * pre_tiles[None, :], "row")
    grad_mine = jnp.sum(grad_total * slots[:, None], axis=0)
    update_mine = jnp.sum(update_total * slots[:, None], axis=0)
    factor = jnp.sqrt(grad_mine) / jnp.sqrt(update_mine + 1e-06)
    return (precond * factor[None, :, None]).astype(jnp.bfloat16).reshape(rows_dev, cols_dev)


def solution(mesh):
    in_specs = (P("row", "col"),)
    out_specs = P("row", "col")
    return jax.shard_map(local, mesh=mesh, in_specs=in_specs, out_specs=out_specs, check_vma=False)
```

profile of v0, /device:TPU:0, one launch (start us, length us, event | category | flops | bytes accessed | tf_op | source)
XLA Modules:
  0.0 498.7 jit_solution(15104935221409702060)
XLA Ops:
  7.4 22.4 %fusion.25 = f32[1536,1536]{1,0:T(8,128)} fusion(bf16[1536,3072]{1,0:T(8,128)(2,1)} %param.1), kind=kOutput, calls=%fused_computation.40 | convolution fusion | flops 14495514624 | bytes 18874368 | tf_op jit(solution)/shard_map/dot_general | solution.py:46
  29.8 0.0 reduce-scatter.2.cloned.1.call-start
  29.8 22.7 %convolution_bitcast_fusion = f32[1536,2,1536]{0,2,1:T(8,128)} fusion(bf16[192,2,8,1536]{3,2,1,0:T(8,128)(2,1)} %bitcast.45), kind=kOutput, calls=%fused_computation.3 | convolution fusion | flops 14495514624 | bytes 28311552 | tf_op jit(solution)/shard_map/rjc,rjd->cjd/dot_general | solution.py:63
  52.6 0.0 reduce-scatter.2.cloned.1.call-update
  52.6 0.2 all-gather.2.cloned.1.call-start
  52.8 1.7 fusion.12
  54.6 276.3 %all-reduce.4.cloned.1.call-done = f32[1536,1536]{1,0:T(8,128)} async-done(((f32[1536,1536]{1,0:T(8,128)}), f32[1536,1536]{1,0:T(8,128)}) %all-reduce.4.cloned.1.call-update) | async-done | bytes 9437200 | tf_op jit(solution)/shard_map/psum | solution.py:50
  330.8 6.8 %multiply_reduce_fusion.2 = f32[]{:T(128)} fusion(f32[1536,1536]{1,0:T(8,128)} %all-reduce.4.cloned.1.call-done), kind=kLoop, calls=%fused_computation.10 | loop fusion | flops 11796479 | bytes 9437188 | tf_op jit(solution)/shard_map/reduce_sum | solution.py:55
  337.6 0.6 fusion.14
  338.3 0.0 reduce-scatter.2.cloned.1.call-done
  338.3 3.1 multiply_reduce_fusion.3
  341.4 6.8 %all-reduce.1 = (f32[4]{0:T(128)S(1)}, f32[2]{0:T(128)S(1)}) all-reduce(f32[4]{0:T(128)S(1)} %fusion.14, f32[2]{0:T(128)S(1)} %multiply_reduce_fusion.3), channel_id=1, replica_groups=mesh['row'=4,'col'=8] {'row'}, use_global_device_ids=true, to_apply=%region_2.3 | all-reduce | flops 6 | bytes 48 | tf_op jit(solution)/shard_map/psum | solution.py:55
  348.2 5.3 %multiply_convert_fusion.2 = bf16[384,2,1536]{0,2,1:T(8,128)(2,1)} fusion(f32[384,2,1536]{0,2,1:T(8,128)} %reduce-scatter.2.cloned.1.call-done, f32[2]{0:T(128)S(1)} %get-tuple-element.16, f32[2]{0:T(128)S(1)} %get-tuple-element.15, f32[384,1536]{0,1:T(8,128)S(1)} %get-tuple-element.12, f32[384,1536]{0,1:T(8,128)} %get-tuple-element.11), kind=kLoop, calls=%fused_computation.16 | loop fusion | flops 5898240 | bytes 11796496 | tf_op jit(solution)/shard_map/convert_element_type | solution.py:80
  353.6 5.6 %multiply_reduce_fusion.1 = f32[3072]{0:T(1024)S(1)} fusion(bf16[1536,3072]{1,0:T(8,128)(2,1)} %param.1), kind=kLoop, calls=%fused_computation.2 | loop fusion | flops 14152704 | bytes 9449472 | tf_op jit(solution)/shard_map/reduce_sum | solution.py:43
  359.2 0.1 reduce_sum.75
  359.3 0.6 select_reduce_fusion
  360.7 55.0 %all-gather.2.cloned.1.call-done = bf16[1536,2,1536]{0,2,1:T(8,128)(2,1)} async-done(((bf16[384,2,1536]{0,2,1:T(8,128)(2,1)}), bf16[1536,2,1536]{0,2,1:T(8,128)(2,1)}) %all-gather.2.cloned.1.call-update) | async-done | bytes 9437200 | tf_op jit(solution)/shard_map/all_gather | solution.py:85
  415.7 21.6 %fusion.3.clone.5 = bf16[1536,2,1536]{0,2,1:T(8,128)(2,1)} fusion(bf16[1536,2,1536]{0,2,1:T(8,128)(2,1)} %all-gather.2.cloned.1.call-done, bf16[192,2,8,1536]{3,2,1,0:T(8,128)(2,1)} %bitcast.46), kind=kOutput, calls=%fused_computation.8.clone.clone.clone.2 | convolution fusion | flops 14500233216 | bytes 28311552 | tf_op jit(solution)/shard_map/rjc,cjd->rjd/dot_general | solution.py:82
  437.3 23.3 %multiply_reduce_fusion = (f32[2]{0:T(128)S(1)}, f32[1536,2,1536]{0,2,1:T(8,128)}) fusion(f32[]{:T(128)S(6)} %mul.126, f32[1536,1536]{1,0:T(8,128)} %all-reduce.4.cloned.1.call-done, f32[]{:T(128)S(6)} %sqrt.16, bf16[1536,2,1536]{0,2,1:T(8,128)(2,1)} %fusion.3.clone.5), kind=kOutput, calls=%fused_computation.1 | convolution fusion | flops 14523826176 | bytes 37748752 | tf_op jit(solution)/shard_map/rk,kjd->rjd/dot_general | solution.py:97
  460.6 0.1 broadcast_multiply_fusion
  460.7 5.9 %all-reduce = (f32[4,2]{0,1:T(2,128)S(1)}, f32[4,2]{0,1:T(2,128)S(1)}) all-reduce(f32[4,2]{0,1:T(2,128)S(1)} %get-tuple-element.14, f32[4,2]{0,1:T(2,128)S(1)} %get-tuple-element.13), channel_id=1, replica_groups=mesh['row'=4,'col'=8] {'row'}, use_global_device_ids=true, to_apply=%region_9.10 | all-reduce | flops 16 | bytes 128 | tf_op jit(solution)/shard_map/psum | solution.py:45
  466.6 0.1 multiply_reduce_fusion.5
  466.8 11.9 %multiply_convert_fusion = bf16[1536,2,1536]{0,2,1:T(8,128)(2,1)} fusion(f32[1536,2,1536]{0,2,1:T(8,128)} %get-tuple-element.18, f32[2]{0:T(128)S(1)} %rsqrt_multiply_fusion), kind=kLoop, calls=%fused_computation | loop fusion | flops 9437184 | bytes 28311560 | tf_op jit(solution)/shard_map/convert_element_type | solution.py:105
  478.7 12.6 %copy.7 = bf16[1536,3072]{1,0:T(8,128)(2,1)} copy(bf16[1536,3072]{0,1:T(8,128)(2,1)} %bitcast.44) | data formatting | bytes 18874368 | tf_op jit(solution)/shard_map/reshape | solution.py:105
  (8 shorter events, 0.1 us)
Async XLA Ops:
  7.4 323.5 %all-reduce.4.cloned.1.call-start = ((), (), s32[]{:S(2)}) async-start(), calls=%async_computation.1 | async-start | bytes 18874368 | tf_op jit(solution)/shard_map/psum | solution.py:50
  29.8 308.5 %reduce-scatter.2.cloned.1.call-start = ((), (), s32[]{:S(2)}) async-start(), calls=%async_computation.2 | async-start | bytes 23592960 | tf_op jit(solution)/shard_map/reduce_scatter | solution.py:62
  52.6 363.1 %all-gather.2.cloned.1.call-start = ((), (), s32[]{:S(2)}) async-start(), calls=%async_computation.3 | async-start | bytes 11796480 | tf_op jit(solution)/shard_map/all_gather | solution.py:85
Sparse Core Ops, SparseCore 0:
  29.9 300.8 all-reduce.3
Sparse Core Ops, SparseCore 1:
  52.7 142.1 reduce-scatter.1
  353.7 62.0 all-gather.1
where the time goes:
time: 499 us
  waiting for transfers between devices  331 us (66%)
  matrix products  90 us (18%)
  other arithmetic  36.1 us (7%)
  between operations  15.6 us (3%)
  blocking collectives  12.7 us (3%)
  local copies, waits for them, and re-layouts  12.6 us (3%)
    psum x1, waiting for transfers between devices, local(): left_rows = lax.psum(left_part, 'col')  276 us
    all_gather x1, waiting for transfers between devices, local(): lax.all_gather(right_piece, 'row', axis=0, tiled=True)  55 us
    dot_general x1, matrix products, local(): jnp.einsum('rk,kjd->rjd', left_root, projected_band, preferred_element_ty...  23.3 us
    dot_general x1, matrix products, local(): jnp.einsum('rjc,rjd->cjd', portion, grad_three, preferred_element_type=jn...  22.7 us
    dot_general x1, matrix products, local(): lax.dot_general(gradient, band, (((1,), (1,)), ((), ())), preferred_eleme...  22.4 us
    dot_general x1, matrix products, local(): jnp.einsum('rjc,cjd->rjd', portion, lax.all_gather(right_piece, 'row', ax...  21.6 us
    reshape x1, local copies, waits for them, and re-layouts, local(): (precond * factor[None, :, None]).astype(jnp.bfloat16)  12.6 us
    convert_element_type x1, other arithmetic, local(): (precond * factor[None, :, None]).astype(jnp.bfloat16)  11.9 us
  transfers between devices with their start and end apart: 3, of which 2 were waited for; matrix products, arithmetic and copies ran while one was open for 8% of the time, Pallas kernels for 0%

commit v1 on v0

--- a/solution.py
+++ b/solution.py
@@ -1,13 +1,21 @@
 import jax
 import jax.numpy as jnp
 from jax import lax
+from jax.experimental import pallas as pl
+from jax.experimental.pallas import tpu as pltpu
 from jax.sharding import PartitionSpec as P
 
 M = 6144
 BLOCK = 1536
+SUB = 256
 
 
 damping = 0.001
+
+STRIPS = BLOCK // SUB
+PAIRS = [(a, b) for a in range(STRIPS) for b in range(a, STRIPS)]
+SLOT = {pair: index for index, pair in enumerate(PAIRS)}
+TRI = len(PAIRS)
 
 
 def swapped(block, axis, apart):
@@ -20,7 +28,7 @@
     return lax.ppermute(block, axis, route)
 
 
-def local(gradient):
+def general(gradient):
     rows_dev, cols_dev = gradient.shape
     col_blocks = cols_dev // BLOCK
     share_count = BLOCK // rows_dev
@@ -105,6 +113,170 @@
     return (precond * factor[None, :, None]).astype(jnp.bfloat16).reshape(rows_dev, cols_dev)
 
 
+def eye():
+    shape = (SUB, SUB)
+    return lax.broadcasted_iota(jnp.int32, shape, 0) == lax.broadcasted_iota(jnp.int32, shape, 1)
+
+
+def store_strip(a, strip, tri_ref, diag_ref):
+    for b in range(a, STRIPS):
+        block = strip[:, (b - a) * SUB : (b - a + 1) * SUB]
+        if a == b:
+            diag_ref[:, a * SUB : (a + 1) * SUB] = jnp.sum(
+                jnp.where(eye(), block, 0.0), axis=0, keepdims=True
+            )
+        tri_ref[SLOT[a, b]] = block.astype(jnp.bfloat16)
+
+
+def left_gram_kernel(g_ref, tri_ref, diag_ref):
+    for a in range(STRIPS):
+        strip = lax.dot_general(
+            g_ref[a * SUB : (a + 1) * SUB, :],
+            g_ref[a * SUB :, :],
+            (((1,), (1,)), ((), ())),
+            preferred_element_type=jnp.float32,
+        )
+        store_strip(a, strip, tri_ref, diag_ref)
+
+
+def right_gram_kernel(g_ref, tri_ref, diag_ref):
+    for a in range(STRIPS):
+        strip = lax.dot_general(
+            g_ref[:, a * SUB : (a + 1) * SUB],
+            g_ref[:, a * SUB :],
+            (((0,), (0,)), ((), ())),
+            preferred_element_type=jnp.float32,
+        )
+        store_strip(a, strip, tri_ref, diag_ref)
+
+
+def build_root(tri_ref, diag_ref, root_ref):
+    diag = diag_ref[...] + damping
+    total = jnp.sum(diag * diag, axis=1, keepdims=True)
+    squares = jnp.zeros((SUB, SUB), jnp.float32)
+    for a, b in PAIRS:
+        block = tri_ref[SLOT[a, b]].astype(jnp.float32)
+        if a == b:
+            block = jnp.where(eye(), 0.0, block)
+            squares = squares + block * block
+        else:
+            squares = squares + 2.0 * (block * block)
+    squares = jnp.sum(jnp.sum(squares, axis=0, keepdims=True), axis=1, keepdims=True)
+    scale = jnp.sqrt(total + squares)
+    inverse = 1.0 / scale
+    gain = 0.25 / jnp.sqrt(jnp.sqrt(scale))
+    on_diag = (5.0 - diag * inverse) * gain
+    for a, b in PAIRS:
+        block = (0.0 - tri_ref[SLOT[a, b]].astype(jnp.float32) * inverse) * gain
+        rows, cols = slice(a * SUB, (a + 1) * SUB), slice(b * SUB, (b + 1) * SUB)
+        if a == b:
+            block = jnp.where(eye(), on_diag[:, cols], block)
+        else:
+            root_ref[cols, rows] = block.T.astype(jnp.bfloat16)
+        root_ref[rows, cols] = block.astype(jnp.bfloat16)
+
+
+CHUNK = 512
+
+
+def apply_kernel(
+    g_ref, left_ref, left_diag, right_ref, right_diag, out_ref, left_root, right_root, proj, pre
+):
+    @pl.when(pl.program_id(0) == 0)
+    def _():
+        build_root(left_ref, left_diag, left_root)
+
+    build_root(right_ref.at[0], right_diag, right_root)
+    zero = jnp.zeros((8, CHUNK), jnp.float32)
+
+    def sums(wide):
+        return jnp.sum((wide * wide).reshape(-1, 8, CHUNK), axis=0)
+
+    def step(n, carry):
+        grad_sum, pre_sum = carry
+        cols = pl.ds(pl.multiple_of(n * CHUNK, CHUNK), CHUNK)
+        proj[...] = jnp.dot(
+            g_ref[...], right_root[:, cols], preferred_element_type=jnp.float32
+        ).astype(jnp.bfloat16)
+        block = jnp.dot(left_root[...], proj[...], preferred_element_type=jnp.float32)
+        pre[:, cols] = block
+        return grad_sum + sums(g_ref[:, cols].astype(jnp.float32)), pre_sum + sums(block)
+
+    grad_sum, pre_sum = lax.fori_loop(0, BLOCK // CHUNK, step, (zero, zero))
+
+    def whole(part):
+        return jnp.sum(jnp.sum(part, axis=0, keepdims=True), axis=1, keepdims=True)
+
+    factor = jnp.sqrt(whole(grad_sum)) / jnp.sqrt(whole(pre_sum) + 1e-06)
+
+    def scale_rows(m, carry):
+        rows = pl.ds(pl.multiple_of(m * SUB, SUB), SUB)
+        out_ref[rows, :] = (pre[rows, :] * factor).astype(jnp.bfloat16)
+        return carry
+
+    lax.fori_loop(0, STRIPS, scale_rows, 0)
+
+
+VMEM_LIMIT = 60 * 1024 * 1024
+
+
+def local(gradient):
+    rows_dev, cols_dev = gradient.shape
+    if rows_dev != BLOCK:
+        return general(gradient)
+    col_blocks = cols_dev // BLOCK
+    params = pltpu.CompilerParams(vmem_limit_bytes=VMEM_LIMIT)
+    flops = BLOCK * BLOCK * cols_dev
+    left_tri, left_diag = pl.pallas_call(
+        left_gram_kernel,
+        out_shape=(
+            jax.ShapeDtypeStruct((TRI, SUB, SUB), jnp.bfloat16),
+            jax.ShapeDtypeStruct((1, BLOCK), jnp.float32),
+        ),
+        compiler_params=params,
+        cost_estimate=pl.CostEstimate(flops=flops, bytes_accessed=13_000_000, transcendentals=0),
+    )(gradient)
+    left_tri = lax.psum(left_tri, "col")
+    left_diag = lax.psum(left_diag, "col")
+    right_tri, right_diag = pl.pallas_call(
+        right_gram_kernel,
+        grid=(col_blocks,),
+        in_specs=[pl.BlockSpec((BLOCK, BLOCK), lambda j: (0, j))],
+        out_specs=(
+            pl.BlockSpec((None, TRI, SUB, SUB), lambda j: (j, 0, 0, 0)),
+            pl.BlockSpec((1, BLOCK), lambda j: (0, j)),
+        ),
+        out_shape=(
+            jax.ShapeDtypeStruct((col_blocks, TRI, SUB, SUB), jnp.bfloat16),
+            jax.ShapeDtypeStruct((1, cols_dev), jnp.float32),
+        ),
+        compiler_params=params,
+        cost_estimate=pl.CostEstimate(flops=flops, bytes_accessed=16_000_000, transcendentals=0),
+    )(gradient)
+    right_tri = lax.psum(right_tri, "row")
+    right_diag = lax.psum(right_diag, "row")
+    return pl.pallas_call(
+        apply_kernel,
+        grid=(col_blocks,),
+        in_specs=[
+            pl.BlockSpec((BLOCK, BLOCK), lambda j: (0, j)),
+            pl.BlockSpec((TRI, SUB, SUB), lambda j: (0, 0, 0)),
+            pl.BlockSpec((1, BLOCK), lambda j: (0, 0)),
+            pl.BlockSpec((1, TRI, SUB, SUB), lambda j: (j, 0, 0, 0)),
+            pl.BlockSpec((1, BLOCK), lambda j: (0, j)),
+        ],
+        out_specs=pl.BlockSpec((BLOCK, BLOCK), lambda j: (0, j)),
+        out_shape=jax.ShapeDtypeStruct((BLOCK, cols_dev), jnp.bfloat16),
+        scratch_shapes=[
+            pltpu.VMEM((BLOCK, BLOCK), jnp.bfloat16),
+            pltpu.VMEM((BLOCK, BLOCK), jnp.bfloat16),
+            pltpu.VMEM((BLOCK, CHUNK), jnp.bfloat16),
+            pltpu.VMEM((BLOCK, BLOCK), jnp.float32),
+        ],
+        compiler_params=params,
+    )(gradient, left_tri, left_diag, right_tri, right_diag)
+
+
 def solution(mesh):
     in_specs = (P("row", "col"),)
     out_specs = P("row", "col")

time: 499 us -> 304 us (0.61)
  waiting for transfers between devices: 331 us -> 180 us
  matrix products: 90 us -> 0 us
  Pallas kernels: 0 us -> 72.5 us
  other arithmetic: 36.1 us -> 0 us
  blocking collectives: 12.7 us -> 36.4 us
  local copies, waits for them, and re-layouts: 12.6 us -> 0.67 us
    psum x1 -> x2, waiting for transfers between devices: 276 us -> 180 us  [the longest x1 108 us: local(): right_tri = lax.psum(right_tri, 'row')]
    dot_general x4 -> x0, matrix products: 90 us -> none  [the longest x1 23.3 us: local(): jnp.einsum('rk,kjd->rjd', left_root, projected_band, preferred_element_ty...]
    pallas_call x0 -> x3, Pallas kernels: none -> 72.5 us  [the longest x1 45.6 us: local(): pl.pallas_call(apply_kernel, grid=(col_blocks,), in_specs=[pl.BlockSpec((...]
    all_gather x1 -> x0, waiting for transfers between devices: 55 us -> none  [local(): lax.all_gather(right_piece, 'row', axis=0, tiled=True)]
    psum x2, blocking collectives: 12.7 us -> 36.4 us  [the longest x1 25.5 us: local(): left_diag = lax.psum(left_diag, 'col')]
    convert_element_type x3 -> x0, other arithmetic: 17.3 us -> none  [the longest x1 11.9 us: local(): (precond * factor[None, :, None]).astype(jnp.bfloat16)]
    reduce_sum x6 -> x0, other arithmetic: 16.4 us -> none  [the longest x1 6.78 us: local(): left_total = lax.psum(slots * jnp.sum(left_rows * left_rows), 'row')]
    reshape x1 -> x0, local copies, waits for them, and re-layouts: 12.6 us -> none  [local(): (precond * factor[None, :, None]).astype(jnp.bfloat16)]
  transfers between devices with their start and end apart: 3 -> 2, of which waited for: 2 -> 2; matrix products, arithmetic and copies ran while one was open for 8% -> 0% of each run, Pallas kernels for 0% -> 4%
where the time goes in v1:
time: 304 us; the launch traced here: 303 us
  waiting for transfers between devices  180 us (59%)
  Pallas kernels  72.5 us (24%)
  blocking collectives  36.4 us (12%)
  between operations  13.4 us (4%)
    psum x1, waiting for transfers between devices, local(): right_tri = lax.psum(right_tri, 'row')  108 us
    psum x1, waiting for transfers between devices, local(): left_tri = lax.psum(left_tri, 'col')  72.1 us
    pallas_call x1, Pallas kernels, local(): pl.pallas_call(apply_kernel, grid=(col_blocks,), in_specs=[pl.BlockSpec((...  45.6 us
    psum x1, blocking collectives, local(): left_diag = lax.psum(left_diag, 'col')  25.5 us
    pallas_call x1, Pallas kernels, local(): pl.pallas_call(left_gram_kernel, out_shape=(jax.ShapeDtypeStruct((TRI, SU...  14 us
    pallas_call x1, Pallas kernels, local(): pl.pallas_call(right_gram_kernel, grid=(col_blocks,), in_specs=[pl.BlockS...  12.8 us
    psum x1, blocking collectives, local(): right_diag = lax.psum(right_diag, 'row')  10.9 us
  transfers between devices with their start and end apart: 2, of which 2 were waited for; matrix products, arithmetic and copies ran while one was open for 0% of the time, Pallas kernels for 4%

profile of v1, /device:TPU:0, one launch (start us, length us, event | category | flops | bytes accessed | tf_op | source)
XLA Modules:
  0.0 303.4 jit_solution(6955420748367119841)
XLA Ops:
  6.5 0.0 all-reduce.3.cloned.1.call-start
  6.5 14.0 %shard_map.17 = (bf16[21,256,256]{2,1,0:T(8,128)(2,1)}, f32[1,1536]{1,0:T(1,128)}) custom-call(bf16[1536,3072]{1,0:T(8,128)(2,1)} %g_ref.5), custom_call_target="tpu_custom_call" | custom-call | flops 7247757312 | bytes 13000000 | tf_op jit(solution)/shard_map/pallas_call | solution.py:230
  20.6 0.0 all-reduce.3.cloned.1.call-update
  20.6 0.0 all-reduce.5.cloned.1.call-start
  20.6 12.8 %shard_map.18 = (bf16[2,21,256,256]{3,2,1,0:T(8,128)(2,1)}, f32[1,3072]{1,0:T(1,128)}) custom-call(bf16[1536,3072]{1,0:T(8,128)(2,1)} %g_ref.5), custom_call_target="tpu_custom_call" | custom-call | flops 7247757312 | bytes 16000000 | tf_op jit(solution)/shard_map/pallas_call | solution.py:241
  33.5 0.0 copy-start.1
  33.5 0.0 copy-start
  33.5 0.0 all-reduce.5.cloned.1.call-update
  33.5 0.7 copy-done.1
  34.2 25.5 %psum.29.left_diag = f32[1,1536]{1,0:T(1,128)} all-reduce(f32[1,1536]{1,0:T(1,128)S(1)} %copy-done.1), channel_id=1, replica_groups=mesh['row'=4,'col'=8] {'col'}, use_global_device_ids=true, to_apply=%region_1.0 | all-reduce | flops 1536 | bytes 12288 | tf_op jit(solution)/shard_map/psum | solution.py:240
  59.6 0.0 copy-done
  59.6 10.9 %psum.31.right_diag = f32[1,3072]{1,0:T(1,128)} all-reduce(f32[1,3072]{1,0:T(1,128)S(1)} %copy-done), channel_id=1, replica_groups=mesh['row'=4,'col'=8] {'row'}, use_global_device_ids=true, to_apply=%region_3.0 | all-reduce | flops 3072 | bytes 24576 | tf_op jit(solution)/shard_map/psum | solution.py:257
  70.5 72.1 %all-reduce.3.cloned.1.call-done.left_ref = bf16[21,256,256]{2,1,0:T(8,128)(2,1)} async-done(((bf16[21,256,256]{2,1,0:T(8,128)(2,1)}), bf16[21,256,256]{2,1,0:T(8,128)(2,1)}) %all-reduce.3.cloned.1.call-update) | async-done | bytes 2752528 | tf_op jit(solution)/shard_map/psum | solution.py:239
  142.7 108.2 %all-reduce.5.cloned.1.call-done.right_ref = bf16[2,21,256,256]{3,2,1,0:T(8,128)(2,1)} async-done(((bf16[2,21,256,256]{3,2,1,0:T(8,128)(2,1)}), bf16[2,21,256,256]{3,2,1,0:T(8,128)(2,1)}) %all-reduce.5.cloned.1.call-update) | async-done | bytes 5505040 | tf_op jit(solution)/shard_map/psum | solution.py:256
  250.9 45.6 %shard_map.19 = bf16[1536,3072]{1,0:T(8,128)(2,1)} custom-call(bf16[1536,3072]{1,0:T(8,128)(2,1)} %g_ref.5, bf16[21,256,256]{2,1,0:T(8,128)(2,1)} %all-reduce.3.cloned.1.call-done.left_ref, f32[1,1536]{1,0:T(1,128)} %psum.29.left_diag, bf16[2,21,256,256]{3,2,1,0:T(8,128)(2,1)} %all-reduce.5.cloned.1.call-done.right_ref, f32[1,3072]{1,0:T(1,128)} %psum.31.right_diag), custom_call_target="tpu_custom_call" | custom-call | tf_op jit(solution)/shard_map/pallas_call | solution.py:258
Async XLA Ops:
  6.5 136.1 %all-reduce.3.cloned.1.call-start = ((), (), s32[]{:S(2)}) async-start(), calls=%async_computation | async-start | bytes 5505024 | tf_op jit(solution)/shard_map/psum | solution.py:239
  20.6 230.3 %all-reduce.5.cloned.1.call-start = ((), (), s32[]{:S(2)}) async-start(), calls=%async_computation.1 | async-start | bytes 11010048 | tf_op jit(solution)/shard_map/psum | solution.py:256
  33.5 0.7 copy-start.1
  33.5 26.2 %copy-start = (f32[1,3072]{1,0:T(1,128)S(1)}, f32[1,3072]{1,0:T(1,128)}, u32[]{:S(2)}) copy-start(f32[1,3072]{1,0:T(1,128)} %get-tuple-element.12) | copy-start | bytes 36868
Sparse Core Ops, SparseCore 0:
  20.7 121.9 all-reduce.2
  145.0 105.8 all-reduce.4

commit v2 on v1

--- a/solution.py
+++ b/solution.py
@@ -16,6 +16,10 @@
 PAIRS = [(a, b) for a in range(STRIPS) for b in range(a, STRIPS)]
 SLOT = {pair: index for index, pair in enumerate(PAIRS)}
 TRI = len(PAIRS)
+TALL = TRI * SUB
+LEFT = TALL // 3
+RIGHT = TALL // 2
+STEP = 224
 
 
 def swapped(block, axis, apart):
@@ -118,36 +122,264 @@
     return lax.broadcasted_iota(jnp.int32, shape, 0) == lax.broadcasted_iota(jnp.int32, shape, 1)
 
 
-def store_strip(a, strip, tri_ref, diag_ref):
-    for b in range(a, STRIPS):
-        block = strip[:, (b - a) * SUB : (b - a + 1) * SUB]
-        if a == b:
-            diag_ref[:, a * SUB : (a + 1) * SUB] = jnp.sum(
-                jnp.where(eye(), block, 0.0), axis=0, keepdims=True
-            )
-        tri_ref[SLOT[a, b]] = block.astype(jnp.bfloat16)
-
-
-def left_gram_kernel(g_ref, tri_ref, diag_ref):
-    for a in range(STRIPS):
+def add_into(dst, dst_at, one, one_at, two, two_at, rows):
+    def piece(m, carry):
+        def part(ref, at):
+            return ref.at[pl.ds(pl.multiple_of(at + m * STEP, 16), STEP), :]
+
+        part(dst, dst_at)[...] = (
+            part(one, one_at)[...].astype(jnp.float32) + part(two, two_at)[...].astype(jnp.float32)
+        ).astype(jnp.bfloat16)
+        return carry
+
+    lax.fori_loop(0, rows // STEP, piece, 0)
+
+
+def gram_kernel(
+    g_ref,
+    left_out,
+    left_diag_out,
+    right_out,
+    right_diag_out,
+    left_part,
+    left_sum,
+    left_y,
+    left_near,
+    left_far,
+    right_part,
+    right_sum,
+    right_core,
+    right_x,
+    left_diag,
+    left_diag_in,
+    right_diag,
+    right_diag_in,
+    send_sem,
+    recv_sem,
+    out_sem,
+):
+    row = lax.axis_index("row")
+    col = lax.axis_index("col")
+
+    def flipped(index, apart):
+        bit = lax.rem(index // apart, 2)
+        return bit, index + apart - 2 * apart * bit
+
+    y_bit, y_mate = flipped(col, 1)
+    near_bit, near_mate = flipped(col, 2)
+    far_bit, far_mate = flipped(col, 4)
+    core_bit, core_mate = flipped(row, 1)
+    _, x_mate = flipped(row, 2)
+    to_y, to_near, to_far = {"col": y_mate}, {"col": near_mate}, {"col": far_mate}
+    to_core, to_x = {"row": core_mate}, {"row": x_mate}
+
+    barrier = pltpu.get_barrier_semaphore()
+    mates = (to_y, to_near, to_far, to_core, to_x)
+    for mate in mates:
+        pl.semaphore_signal(barrier, inc=1, device_id=mate, device_id_type=pl.DeviceIdType.MESH)
+
+    copies = {}
+
+    def send(name, src, dst, mate):
+        index = len(copies)
+        copy = pltpu.make_async_remote_copy(
+            src_ref=src,
+            dst_ref=dst,
+            send_sem=send_sem.at[index],
+            recv_sem=recv_sem.at[index],
+            device_id=mate,
+            device_id_type=pl.DeviceIdType.MESH,
+        )
+        copy.start()
+        copies[name] = copy
+
+    def got(name):
+        copies[name].wait_recv()
+
+    outs = []
+
+    def emit(src, dst):
+        copy = pltpu.make_async_copy(src, dst, out_sem.at[len(outs)])
+        copy.start()
+        outs.append(copy)
+
+    def rows(ref, at, count):
+        return ref.at[pl.ds(pl.multiple_of(at, 16), count), :]
+
+    def store_strip(a, strip, part, base, diag, diag_base):
+        for b in range(a, STRIPS):
+            block = strip[:, (b - a) * SUB : (b - a + 1) * SUB]
+            if a == b:
+                diag[:, diag_base + a * SUB : diag_base + (a + 1) * SUB] = jnp.sum(
+                    jnp.where(eye(), block, 0.0), axis=0, keepdims=True
+                )
+            at = base + SLOT[a, b] * SUB
+            part[at : at + SUB, :] = block.astype(jnp.bfloat16)
+
+    def left_strip(a):
         strip = lax.dot_general(
             g_ref[a * SUB : (a + 1) * SUB, :],
             g_ref[a * SUB :, :],
             (((1,), (1,)), ((), ())),
             preferred_element_type=jnp.float32,
         )
-        store_strip(a, strip, tri_ref, diag_ref)
-
-
-def right_gram_kernel(g_ref, tri_ref, diag_ref):
-    for a in range(STRIPS):
+        store_strip(a, strip, left_part, 0, left_diag.at[0], 0)
+
+    def right_strip(j, a):
+        low, high = j * BLOCK + a * SUB, (j + 1) * BLOCK
         strip = lax.dot_general(
-            g_ref[:, a * SUB : (a + 1) * SUB],
-            g_ref[:, a * SUB :],
+            g_ref[:, low : low + SUB],
+            g_ref[:, low:high],
             (((0,), (0,)), ((), ())),
             preferred_element_type=jnp.float32,
         )
-        store_strip(a, strip, tri_ref, diag_ref)
+        store_strip(a, strip, right_part, j * TALL, right_diag.at[0], j * BLOCK)
+
+    half, quarter, eighth = LEFT // 2, LEFT // 4, LEFT // 8
+
+    def at_y(c):
+        return c * LEFT + y_bit * half
+
+    def at_near(c):
+        return at_y(c) + near_bit * quarter
+
+    def at_far(c):
+        return at_near(c) + far_bit * eighth
+
+    def y_send(c):
+        send(("y", c), rows(left_part, c * LEFT + (1 - y_bit) * half, half),
+             rows(left_y, c * half, half), to_y)
+
+    def near_send(c):
+        got(("y", c))
+        add_into(left_part, at_y(c), left_part, at_y(c), left_y, c * half, half)
+        send(("near", c), rows(left_part, at_y(c) + (1 - near_bit) * quarter, quarter),
+             rows(left_near, c * quarter, quarter), to_near)
+
+    def far_send(c):
+        got(("near", c))
+        add_into(left_part, at_near(c), left_part, at_near(c), left_near, c * quarter, quarter)
+        send(("far", c), rows(left_part, at_near(c) + (1 - far_bit) * eighth, eighth),
+             rows(left_far, c * eighth, eighth), to_far)
+
+    def far_back(c):
+        got(("far", c))
+        add_into(left_sum, at_far(c), left_part, at_far(c), left_far, c * eighth, eighth)
+        mine = rows(left_sum, at_far(c), eighth)
+        send(("far_back", c), mine, mine, to_far)
+
+    def near_back(c):
+        got(("far_back", c))
+        mine = rows(left_sum, at_near(c), quarter)
+        send(("near_back", c), mine, mine, to_near)
+
+    def y_back(c):
+        got(("near_back", c))
+        mine = rows(left_sum, at_y(c), half)
+        send(("y_back", c), mine, mine, to_y)
+
+    def left_done(c):
+        got(("y_back", c))
+        emit(rows(left_sum, c * LEFT, LEFT), rows(left_out, c * LEFT, LEFT))
+
+    share = RIGHT // 2
+
+    def at_core(k):
+        return k * RIGHT + core_bit * share
+
+    def core_send(k):
+        send(("core", k), rows(right_part, k * RIGHT + (1 - core_bit) * share, share),
+             rows(right_core, k * share, share), to_core)
+
+    def x_send(k):
+        got(("core", k))
+        add_into(right_part, at_core(k), right_part, at_core(k), right_core, k * share, share)
+        send(("x", k), rows(right_part, at_core(k), share), rows(right_x, k * share, share), to_x)
+
+    def core_back(k):
+        got(("x", k))
+        add_into(right_sum, at_core(k), right_part, at_core(k), right_x, k * share, share)
+        mine = rows(right_sum, at_core(k), share)
+        send(("core_back", k), mine, mine, to_core)
+
+    def right_done(k):
+        got(("core_back", k))
+        emit(rows(right_sum, k * RIGHT, RIGHT), rows(right_out, k * RIGHT, RIGHT))
+
+    def diag_send(name, slot, own, landing, mate):
+        send(("diag", name), own.at[slot], landing.at[slot], mate)
+
+    def diag_add(name, slot, own, landing):
+        got(("diag", name))
+        own[slot + 1] = own[slot] + landing[slot]
+
+    left_strip(0)
+    left_strip(1)
+    pl.semaphore_wait(barrier, len(mates))
+    y_send(0)
+    left_strip(2)
+    y_send(1)
+    for a in range(3, STRIPS):
+        left_strip(a)
+    y_send(2)
+    diag_send("y", 0, left_diag, left_diag_in, to_y)
+    right_strip(0, 0)
+    right_strip(0, 1)
+    core_send(0)
+    near_send(0)
+    for a in range(2, STRIPS):
+        right_strip(0, a)
+    core_send(1)
+    x_send(0)
+    far_send(0)
+    right_strip(1, 0)
+    right_strip(1, 1)
+    core_send(2)
+    x_send(1)
+    near_send(1)
+    for a in range(2, STRIPS):
+        right_strip(1, a)
+    core_send(3)
+    diag_send("core", 0, right_diag, right_diag_in, to_core)
+    x_send(2)
+    x_send(3)
+    far_back(0)
+    diag_add("y", 0, left_diag, left_diag_in)
+    diag_send("near", 1, left_diag, left_diag_in, to_near)
+    diag_add("core", 0, right_diag, right_diag_in)
+    diag_send("x", 1, right_diag, right_diag_in, to_x)
+    far_send(1)
+    near_back(0)
+    near_send(2)
+    diag_add("near", 1, left_diag, left_diag_in)
+    diag_send("far", 2, left_diag, left_diag_in, to_far)
+    far_back(1)
+    y_back(0)
+    far_send(2)
+    core_back(0)
+    near_back(1)
+    far_back(2)
+    y_back(1)
+    near_back(2)
+    diag_add("x", 1, right_diag, right_diag_in)
+    diag_add("far", 2, left_diag, left_diag_in)
+    left_diag_out[...] = left_diag[3]
+    right_diag_out[...] = right_diag[2]
+    core_back(1)
+    left_done(0)
+    y_back(2)
+    right_done(0)
+    left_done(1)
+    core_back(2)
+    right_done(1)
+    left_done(2)
+    core_back(3)
+    right_done(2)
+    right_done(3)
+    for copy in copies.values():
+        copy.wait_send()
+    for copy in outs:
+        copy.wait()
 
 
 def build_root(tri_ref, diag_ref, root_ref):
@@ -155,7 +387,7 @@
     total = jnp.sum(diag * diag, axis=1, keepdims=True)
     squares = jnp.zeros((SUB, SUB), jnp.float32)
     for a, b in PAIRS:
-        block = tri_ref[SLOT[a, b]].astype(jnp.float32)
+        block = tri_ref[SLOT[a, b] * SUB : (SLOT[a, b] + 1) * SUB, :].astype(jnp.float32)
         if a == b:
             block = jnp.where(eye(), 0.0, block)
             squares = squares + block * block
@@ -167,7 +399,7 @@
     gain = 0.25 / jnp.sqrt(jnp.sqrt(scale))
     on_diag = (5.0 - diag * inverse) * gain
     for a, b in PAIRS:
-        block = (0.0 - tri_ref[SLOT[a, b]].astype(jnp.float32) * inverse) * gain
+        block = (0.0 - tri_ref[SLOT[a, b] * SUB : (SLOT[a, b] + 1) * SUB, :].astype(jnp.float32) * inverse) * gain
         rows, cols = slice(a * SUB, (a + 1) * SUB), slice(b * SUB, (b + 1) * SUB)
         if a == b:
             block = jnp.where(eye(), on_diag[:, cols], block)
@@ -186,7 +418,7 @@
     def _():
         build_root(left_ref, left_diag, left_root)
 
-    build_root(right_ref.at[0], right_diag, right_root)
+    build_root(right_ref, right_diag, right_root)
     zero = jnp.zeros((8, CHUNK), jnp.float32)
 
     def sums(wide):
@@ -222,47 +454,55 @@
 
 def local(gradient):
     rows_dev, cols_dev = gradient.shape
-    if rows_dev != BLOCK:
+    if (rows_dev, cols_dev) != (BLOCK, 2 * BLOCK) or (
+        (lax.axis_size("row"), lax.axis_size("col")) != (4, 8)
+    ):
         return general(gradient)
     col_blocks = cols_dev // BLOCK
     params = pltpu.CompilerParams(vmem_limit_bytes=VMEM_LIMIT)
-    flops = BLOCK * BLOCK * cols_dev
-    left_tri, left_diag = pl.pallas_call(
-        left_gram_kernel,
+    vmem = pl.BlockSpec(memory_space=pltpu.VMEM)
+    anywhere = pl.BlockSpec(memory_space=pl.ANY)
+    half = jnp.bfloat16
+    left_tri, left_diag, right_tri, right_diag = pl.pallas_call(
+        gram_kernel,
+        in_specs=[vmem],
+        out_specs=(anywhere, vmem, anywhere, vmem),
         out_shape=(
-            jax.ShapeDtypeStruct((TRI, SUB, SUB), jnp.bfloat16),
+            jax.ShapeDtypeStruct((TALL, SUB), half),
             jax.ShapeDtypeStruct((1, BLOCK), jnp.float32),
-        ),
-        compiler_params=params,
-        cost_estimate=pl.CostEstimate(flops=flops, bytes_accessed=13_000_000, transcendentals=0),
-    )(gradient)
-    left_tri = lax.psum(left_tri, "col")
-    left_diag = lax.psum(left_diag, "col")
-    right_tri, right_diag = pl.pallas_call(
-        right_gram_kernel,
-        grid=(col_blocks,),
-        in_specs=[pl.BlockSpec((BLOCK, BLOCK), lambda j: (0, j))],
-        out_specs=(
-            pl.BlockSpec((None, TRI, SUB, SUB), lambda j: (j, 0, 0, 0)),
-            pl.BlockSpec((1, BLOCK), lambda j: (0, j)),
-        ),
-        out_shape=(
-            jax.ShapeDtypeStruct((col_blocks, TRI, SUB, SUB), jnp.bfloat16),
+            jax.ShapeDtypeStruct((col_blocks * TALL, SUB), half),
             jax.ShapeDtypeStruct((1, cols_dev), jnp.float32),
         ),
-        compiler_params=params,
-        cost_estimate=pl.CostEstimate(flops=flops, bytes_accessed=16_000_000, transcendentals=0),
+        scratch_shapes=[
+            pltpu.VMEM((TALL, SUB), half),
+            pltpu.VMEM((TALL, SUB), half),
+            pltpu.VMEM((TALL // 2, SUB), half),
+            pltpu.VMEM((TALL // 4, SUB), half),
+            pltpu.VMEM((TALL // 8, SUB), half),
+            pltpu.VMEM((col_blocks * TALL, SUB), half),
+            pltpu.VMEM((col_blocks * TALL, SUB), half),
+            pltpu.VMEM((col_blocks * TALL // 2, SUB), half),
+            pltpu.VMEM((col_blocks * TALL // 2, SUB), half),
+            pltpu.VMEM((4, 1, BLOCK), jnp.float32),
+            pltpu.VMEM((3, 1, BLOCK), jnp.float32),
+            pltpu.VMEM((3, 1, cols_dev), jnp.float32),
+            pltpu.VMEM((2, 1, cols_dev), jnp.float32),
+            pltpu.SemaphoreType.DMA((35,)),
+            pltpu.SemaphoreType.DMA((35,)),
+            pltpu.SemaphoreType.DMA((7,)),
+        ],
+        compiler_params=pltpu.CompilerParams(
+            vmem_limit_bytes=VMEM_LIMIT, collective_id=0, has_side_effects=True
+        ),
     )(gradient)
-    right_tri = lax.psum(right_tri, "row")
-    right_diag = lax.psum(right_diag, "row")
     return pl.pallas_call(
         apply_kernel,
         grid=(col_blocks,),
         in_specs=[
             pl.BlockSpec((BLOCK, BLOCK), lambda j: (0, j)),
-            pl.BlockSpec((TRI, SUB, SUB), lambda j: (0, 0, 0)),
+            pl.BlockSpec((TALL, SUB), lambda j: (0, 0)),
             pl.BlockSpec((1, BLOCK), lambda j: (0, 0)),
-            pl.BlockSpec((1, TRI, SUB, SUB), lambda j: (j, 0, 0, 0)),
+            pl.BlockSpec((TALL, SUB), lambda j: (j, 0)),
             pl.BlockSpec((1, BLOCK), lambda j: (0, j)),
         ],
         out_specs=pl.BlockSpec((BLOCK, BLOCK), lambda j: (0, j)),

time: 304 us -> 145 us (0.48)
  waiting for transfers between devices: 180 us -> 0 us
  Pallas kernels: 72.5 us -> 144 us
  blocking collectives: 36.4 us -> 0 us
  between operations: 13.4 us -> 0.01 us
    psum x2 -> x0, waiting for transfers between devices: 180 us -> none  [the longest x1 108 us: local(): right_tri = lax.psum(right_tri, 'row')]
    pallas_call x2 -> x1, Pallas kernels: 26.9 us -> 98.1 us  [local(): pl.pallas_call(gram_kernel, in_specs=[vmem], out_specs=(anywhere, vmem, a...]
    psum x2 -> x0, blocking collectives: 36.4 us -> none  [the longest x1 25.5 us: local(): left_diag = lax.psum(left_diag, 'col')]
  transfers between devices with their start and end apart: 2 -> 0, of which waited for: 2 -> 0; matrix products, arithmetic and copies ran while one was open for 0% -> 0% of each run, Pallas kernels for 4% -> 0%
where the time goes in v2:
time: 145 us; the launch traced here: 144 us
  Pallas kernels  144 us (99%)
    pallas_call x1, Pallas kernels, local(): pl.pallas_call(gram_kernel, in_specs=[vmem], out_specs=(anywhere, vmem, a...  98.1 us
    pallas_call x1, Pallas kernels, local(): pl.pallas_call(apply_kernel, grid=(col_blocks,), in_specs=[pl.BlockSpec((...  45.9 us

profile of v2, /device:TPU:0, one launch (start us, length us, event | category | flops | bytes accessed | tf_op | source)
XLA Modules:
  0.0 144.0 jit_solution(8439095255752648615)
XLA Ops:
  0.0 98.1 %shard_map.17 = (bf16[5376,256]{1,0:T(8,128)(2,1)}, f32[1,1536]{1,0:T(1,128)}, bf16[10752,256]{1,0:T(8,128)(2,1)}, f32[1,3072]{1,0:T(1,128)}) custom-call(bf16[1536,3072]{1,0:T(8,128)(2,1)} %g_ref.3), custom_call_target="tpu_custom_call" | custom-call | tf_op jit(solution)/shard_map/pallas_call | solution.py:466
  98.1 45.9 %shard_map.18 = bf16[1536,3072]{1,0:T(8,128)(2,1)} custom-call(bf16[1536,3072]{1,0:T(8,128)(2,1)} %g_ref.3, bf16[5376,256]{1,0:T(8,128)(2,1)} %get-tuple-element.9.left_ref, f32[1,1536]{1,0:T(1,128)} %get-tuple-element.10.left_diag, bf16[10752,256]{1,0:T(8,128)(2,1)} %get-tuple-element.11.right_ref, f32[1,3072]{1,0:T(1,128)} %get-tuple-element.12.right_diag), custom_call_target="tpu_custom_call" | custom-call | tf_op jit(solution)/shard_map/pallas_call | solution.py:498

commit v3 on v2

v3 whole, which is shorter than its diff:
```python
import jax
import jax.numpy as jnp
from jax import lax
from jax.experimental import pallas as pl
from jax.experimental.pallas import tpu as pltpu
from jax.sharding import PartitionSpec as P

M = 6144
BLOCK = 1536
SUB = 256


damping = 0.001

STRIPS = BLOCK // SUB
PAIRS = [(a, b) for a in range(STRIPS) for b in range(a, STRIPS)]
SLOT = {pair: index for index, pair in enumerate(PAIRS)}
TRI = len(PAIRS)
TALL = TRI * SUB
LEFT = TALL // 3
RIGHT = TALL // 2
STEP = 224


def swapped(block, axis, apart):
    count = lax.axis_size(axis)
    route = []
    for low in range(count):
        high = low | 1 << apart
        if high != low and high < count:
            route += [(low, high), (high, low)]
    return lax.ppermute(block, axis, route)


def general(gradient):
    rows_dev, cols_dev = gradient.shape
    col_blocks = cols_dev // BLOCK
    share_count = BLOCK // rows_dev
    sections = share_count.bit_length() - 1
    row_count = lax.axis_size("row")
    row_index = lax.axis_index("row")
    row_blocks = M // BLOCK
    my_block = row_index // share_count
    offset = row_index % share_count * rows_dev
    slots = (jnp.arange(row_blocks) == my_block).astype(jnp.float32)
    band = gradient
    for bit in range(sections):
        partner = swapped(band, "row", bit)
        upper = row_index // 2**bit % 2 == 1
        band = jnp.where(
            upper, jnp.concatenate([partner, band], 0), jnp.concatenate([band, partner], 0)
        )
    grad_three = gradient.reshape(rows_dev, col_blocks, BLOCK)
    grad_wide = grad_three.astype(jnp.float32)
    grad_tiles = jnp.sum(grad_wide * grad_wide, axis=(0, 2))
    grad_slots = slots[:, None] * grad_tiles[None, :]
    grad_total = lax.psum(grad_slots, "row")
    left_part = lax.dot_general(
        gradient, band, (((1,), (1,)), ((), ())), preferred_element_type=jnp.float32
    )
    row_place = offset + lax.broadcasted_iota(jnp.int32, (rows_dev, 1), 0)
    left_rows = lax.psum(left_part, "col")
    diagonal = (lax.broadcasted_iota(jnp.int32, (rows_dev, BLOCK), 1) == row_place).astype(
        jnp.float32
    )
    left_rows = left_rows + damping * diagonal
    left_total = lax.psum(slots * jnp.sum(left_rows * left_rows), "row")
    left_scale = jnp.sqrt(jnp.sum(left_total * slots))
    left_root = ((5.0 * diagonal - left_rows / left_scale) * 0.25 * left_scale ** (-0.25)).astype(
        jnp.bfloat16
    )
    right_rows = BLOCK // row_count
    portion = grad_three
    right_share = lax.psum_scatter(
        jnp.einsum("rjc,rjd->cjd", portion, grad_three, preferred_element_type=jnp.float32),
        "row",
        scatter_dimension=0,
        tiled=True,
    )
    right_place = row_index * right_rows + lax.broadcasted_iota(
        jnp.int32, (right_rows, 1, BLOCK), 0
    )
    right_diagonal = (
        lax.broadcasted_iota(jnp.int32, (right_rows, 1, BLOCK), 2) == right_place
    ).astype(jnp.float32)
    right_share = right_share + damping * right_diagonal
    right_squares = jnp.sum(right_share * right_share, axis=(0, 2))
    right_total = lax.psum(right_squares, "row")
    right_scale = jnp.sqrt(right_total)[None, :, None]
    right_piece = (
        (5.0 * right_diagonal - right_share / right_scale) * 0.25 * right_scale ** (-0.25)
    ).astype(jnp.bfloat16)
    portion = grad_three
    projected = jnp.einsum(
        "rjc,cjd->rjd",
        portion,
        lax.all_gather(right_piece, "row", axis=0, tiled=True),
        preferred_element_type=jnp.float32,
    ).astype(jnp.bfloat16)
    projected_band = projected
    for bit in range(sections):
        partner_rows = swapped(projected_band, "row", bit)
        upper = row_index // 2**bit % 2 == 1
        projected_band = jnp.where(
            upper,
            jnp.concatenate([partner_rows, projected_band], 0),
            jnp.concatenate([projected_band, partner_rows], 0),
        )
    precond = jnp.einsum(
        "rk,kjd->rjd", left_root, projected_band, preferred_element_type=jnp.float32
    )
    pre_tiles = jnp.sum(precond * precond, axis=(0, 2))
    update_total = lax.psum(slots[:, None] * pre_tiles[None, :], "row")
    grad_mine = jnp.sum(grad_total * slots[:, None], axis=0)
    update_mine = jnp.sum(update_total * slots[:, None], axis=0)
    factor = jnp.sqrt(grad_mine) / jnp.sqrt(update_mine + 1e-06)
    return (precond * factor[None, :, None]).astype(jnp.bfloat16).reshape(rows_dev, cols_dev)


def eye():
    shape = (SUB, SUB)
    return lax.broadcasted_iota(jnp.int32, shape, 0) == lax.broadcasted_iota(jnp.int32, shape, 1)


def add_into(dst, dst_at, one, one_at, two, two_at, rows):
    def piece(m, carry):
        def part(ref, at):
            return ref.at[pl.ds(pl.multiple_of(at + m * STEP, 16), STEP), :]

        part(dst, dst_at)[...] = (
            part(one, one_at)[...].astype(jnp.float32) + part(two, two_at)[...].astype(jnp.float32)
        ).astype(jnp.bfloat16)
        return carry

    lax.fori_loop(0, rows // STEP, piece, 0)


def build_root(tri_ref, diag_ref, root_ref):
    diag = diag_ref[...] + damping
    total = jnp.sum(diag * diag, axis=1, keepdims=True)
    squares = jnp.zeros((SUB, SUB), jnp.float32)
    for a, b in PAIRS:
        block = tri_ref[SLOT[a, b] * SUB : (SLOT[a, b] + 1) * SUB, :].astype(jnp.float32)
        if a == b:
            block = jnp.where(eye(), 0.0, block)
            squares = squares + block * block
        else:
            squares = squares + 2.0 * (block * block)
    squares = jnp.sum(jnp.sum(squares, axis=0, keepdims=True), axis=1, keepdims=True)
    scale = jnp.sqrt(total + squares)
    inverse = 1.0 / scale
    gain = 0.25 / jnp.sqrt(jnp.sqrt(scale))
    on_diag = (5.0 - diag * inverse) * gain
    for a, b in PAIRS:
        block = (0.0 - tri_ref[SLOT[a, b] * SUB : (SLOT[a, b] + 1) * SUB, :].astype(jnp.float32) * inverse) * gain
        rows, cols = slice(a * SUB, (a + 1) * SUB), slice(b * SUB, (b + 1) * SUB)
        if a == b:
            block = jnp.where(eye(), on_diag[:, cols], block)
        else:
            root_ref[cols, rows] = block.T.astype(jnp.bfloat16)
        root_ref[rows, cols] = block.astype(jnp.bfloat16)


CHUNK = 512


def gram_kernel(
    g_ref,
    left_out,
    left_diag_out,
    grad_out,
    proj_out,
    left_part,
    left_sum,
    left_y,
    left_near,
    left_far,
    right_part,
    right_sum,
    right_core,
    right_x,
    left_diag,
    left_diag_in,
    right_diag,
    right_diag_in,
    right_root,
    proj,
    send_sem,
    recv_sem,
    out_sem,
):
    row = lax.axis_index("row")
    col = lax.axis_index("col")

    def flipped(index, apart):
        bit = lax.rem(index // apart, 2)
        return bit, index + apart - 2 * apart * bit

    y_bit, y_mate = flipped(col, 1)
    near_bit, near_mate = flipped(col, 2)
    far_bit, far_mate = flipped(col, 4)
    core_bit, core_mate = flipped(row, 1)
    _, x_mate = flipped(row, 2)
    to_y, to_near, to_far = {"col": y_mate}, {"col": near_mate}, {"col": far_mate}
    to_core, to_x = {"row": core_mate}, {"row": x_mate}

    barrier = pltpu.get_barrier_semaphore()
    mates = (to_y, to_near, to_far, to_core, to_x)
    for mate in mates:
        pl.semaphore_signal(barrier, inc=1, device_id=mate, device_id_type=pl.DeviceIdType.MESH)

    copies = {}

    def send(name, src, dst, mate):
        index = len(copies)
        copy = pltpu.make_async_remote_copy(
            src_ref=src,
            dst_ref=dst,
            send_sem=send_sem.at[index],
            recv_sem=recv_sem.at[index],
            device_id=mate,
            device_id_type=pl.DeviceIdType.MESH,
        )
        copy.start()
        copies[name] = copy

    def got(name):
        copies[name].wait_recv()

    outs = []

    def emit(src, dst):
        copy = pltpu.make_async_copy(src, dst, out_sem.at[len(outs)])
        copy.start()
        outs.append(copy)

    def rows(ref, at, count):
        return ref.at[pl.ds(pl.multiple_of(at, 16), count), :]

    def store_strip(a, strip, part, base, diag, diag_base):
        for b in range(a, STRIPS):
            block = strip[:, (b - a) * SUB : (b - a + 1) * SUB]
            if a == b:
                diag[:, diag_base + a * SUB : diag_base + (a + 1) * SUB] = jnp.sum(
                    jnp.where(eye(), block, 0.0), axis=0, keepdims=True
                )
            at = base + SLOT[a, b] * SUB
            part[at : at + SUB, :] = block.astype(jnp.bfloat16)

    def left_strip(a):
        strip = lax.dot_general(
            g_ref[a * SUB : (a + 1) * SUB, :],
            g_ref[a * SUB :, :],
            (((1,), (1,)), ((), ())),
            preferred_element_type=jnp.float32,
        )
        store_strip(a, strip, left_part, 0, left_diag.at[0], 0)

    def right_strip(j, a):
        low, high = j * BLOCK + a * SUB, (j + 1) * BLOCK
        strip = lax.dot_general(
            g_ref[:, low : low + SUB],
            g_ref[:, low:high],
            (((0,), (0,)), ((), ())),
            preferred_element_type=jnp.float32,
        )
        store_strip(a, strip, right_part, j * TALL, right_diag.at[0], j * BLOCK)

    half, quarter, eighth = LEFT // 2, LEFT // 4, LEFT // 8

    def at_y(c):
        return c * LEFT + y_bit * half

    def at_near(c):
        return at_y(c) + near_bit * quarter

    def at_far(c):
        return at_near(c) + far_bit * eighth

    def y_send(c):
        send(("y", c), rows(left_part, c * LEFT + (1 - y_bit) * half, half),
             rows(left_y, c * half, half), to_y)

    def near_send(c):
        got(("y", c))
        add_into(left_part, at_y(c), left_part, at_y(c), left_y, c * half, half)
        send(("near", c), rows(left_part, at_y(c) + (1 - near_bit) * quarter, quarter),
             rows(left_near, c * quarter, quarter), to_near)

    def far_send(c):
        got(("near", c))
        add_into(left_part, at_near(c), left_part, at_near(c), left_near, c * quarter, quarter)
        send(("far", c), rows(left_part, at_near(c) + (1 - far_bit) * eighth, eighth),
             rows(left_far, c * eighth, eighth), to_far)

    def far_back(c):
        got(("far", c))
        add_into(left_sum, at_far(c), left_part, at_far(c), left_far, c * eighth, eighth)
        mine = rows(left_sum, at_far(c), eighth)
        send(("far_back", c), mine, mine, to_far)

    def near_back(c):
        got(("far_back", c))
        mine = rows(left_sum, at_near(c), quarter)
        send(("near_back", c), mine, mine, to_near)

    def y_back(c):
        got(("near_back", c))
        mine = rows(left_sum, at_y(c), half)
        send(("y_back", c), mine, mine, to_y)

    def left_done(c):
        got(("y_back", c))
        emit(rows(left_sum, c * LEFT, LEFT), rows(left_out, c * LEFT, LEFT))

    share = RIGHT // 2

    def at_core(k):
        return k * RIGHT + core_bit * share

    def core_send(k):
        send(("core", k), rows(right_part, k * RIGHT + (1 - core_bit) * share, share),
             rows(right_core, k * share, share), to_core)

    def x_send(k):
        got(("core", k))
        add_into(right_part, at_core(k), right_part, at_core(k), right_core, k * share, share)
        send(("x", k), rows(right_part, at_core(k), share), rows(right_x, k * share, share), to_x)

    def core_back(k):
        got(("x", k))
        add_into(right_sum, at_core(k), right_part, at_core(k), right_x, k * share, share)
        mine = rows(right_sum, at_core(k), share)
        send(("core_back", k), mine, mine, to_core)

    def diag_send(name, slot, own, landing, mate):
        send(("diag", name), own.at[slot], landing.at[slot], mate)

    def diag_add(name, slot, own, landing):
        got(("diag", name))
        own[slot + 1] = own[slot] + landing[slot]

    def project(j, n):
        low = j * BLOCK + n * CHUNK
        proj[:, low : low + CHUNK] = jnp.dot(
            g_ref[:, j * BLOCK : (j + 1) * BLOCK],
            right_root[:, n * CHUNK : (n + 1) * CHUNK],
            preferred_element_type=jnp.float32,
        ).astype(jnp.bfloat16)

    def right_ready(j):
        got(("core_back", 2 * j))
        got(("core_back", 2 * j + 1))
        build_root(
            right_sum.at[j * TALL : (j + 1) * TALL, :],
            right_diag.at[2, :, j * BLOCK : (j + 1) * BLOCK],
            right_root,
        )

    def emit_proj(j):
        cols = slice(j * BLOCK, (j + 1) * BLOCK)
        emit(proj.at[:, cols], proj_out.at[:, cols])

    right_strip(0, 0)
    right_strip(0, 1)
    pl.semaphore_wait(barrier, len(mates))
    core_send(0)
    left_strip(0)
    x_send(0)
    left_strip(1)
    y_send(0)
    for a in range(2, STRIPS):
        right_strip(0, a)
    core_send(1)
    left_strip(2)
    y_send(1)
    x_send(1)
    for a in range(3, STRIPS):
        left_strip(a)
    y_send(2)
    diag_send("y", 0, left_diag, left_diag_in, to_y)
    near_send(0)
    right_strip(1, 0)
    right_strip(1, 1)
    core_send(2)
    for a in range(2, STRIPS):
        right_strip(1, a)
    core_send(3)
    diag_send("core", 0, right_diag, right_diag_in, to_core)
    grad_out[...] = right_diag[0]
    far_send(0)
    x_send(2)
    core_back(0)
    near_send(1)
    x_send(3)
    diag_add("y", 0, left_diag, left_diag_in)
    diag_send("near", 1, left_diag, left_diag_in, to_near)
    diag_add("core", 0, right_diag, right_diag_in)
    diag_send("x", 1, right_diag, right_diag_in, to_x)
    far_back(0)
    far_send(1)
    core_back(1)
    diag_add("x", 1, right_diag, right_diag_in)
    diag_add("near", 1, left_diag, left_diag_in)
    diag_send("far", 2, left_diag, left_diag_in, to_far)
    near_back(0)
    near_send(2)
    right_ready(0)
    far_back(1)
    y_back(0)
    far_send(2)
    project(0, 0)
    near_back(1)
    project(0, 1)
    far_back(2)
    y_back(1)
    core_back(2)
    project(0, 2)
    emit_proj(0)
    near_back(2)
    diag_add("far", 2, left_diag, left_diag_in)
    left_diag_out[...] = left_diag[3]
    left_done(0)
    y_back(2)
    core_back(3)
    left_done(1)
    right_ready(1)
    project(1, 0)
    left_done(2)
    project(1, 1)
    project(1, 2)
    emit_proj(1)
    for copy in copies.values():
        copy.wait_send()
    for copy in outs:
        copy.wait()


def apply_kernel(proj_ref, grad_ref, left_ref, left_diag, out_ref, left_root, pre):
    @pl.when(pl.program_id(0) == 0)
    def _():
        build_root(left_ref, left_diag, left_root)

    def step(n, pre_sum):
        cols = pl.ds(pl.multiple_of(n * CHUNK, CHUNK), CHUNK)
        block = jnp.dot(left_root[...], proj_ref[:, cols], preferred_element_type=jnp.float32)
        pre[:, cols] = block
        return pre_sum + jnp.sum((block * block).reshape(-1, 8, CHUNK), axis=0)

    pre_sum = lax.fori_loop(0, BLOCK // CHUNK, step, jnp.zeros((8, CHUNK), jnp.float32))
    pre_sum = jnp.sum(jnp.sum(pre_sum, axis=0, keepdims=True), axis=1, keepdims=True)
    grad_sum = jnp.sum(grad_ref[...], axis=1, keepdims=True)
    factor = jnp.sqrt(grad_sum) / jnp.sqrt(pre_sum + 1e-06)

    def scale_rows(m, carry):
        rows = pl.ds(pl.multiple_of(m * SUB, SUB), SUB)
        out_ref[rows, :] = (pre[rows, :] * factor).astype(jnp.bfloat16)
        return carry

    lax.fori_loop(0, STRIPS, scale_rows, 0)


VMEM_LIMIT = 60 * 1024 * 1024


def local(gradient):
    rows_dev, cols_dev = gradient.shape
    if (rows_dev, cols_dev) != (BLOCK, 2 * BLOCK) or (
        (lax.axis_size("row"), lax.axis_size("col")) != (4, 8)
    ):
        return general(gradient)
    col_blocks = cols_dev // BLOCK
    params = pltpu.CompilerParams(vmem_limit_bytes=VMEM_LIMIT)
    vmem = pl.BlockSpec(memory_space=pltpu.VMEM)
    anywhere = pl.BlockSpec(memory_space=pl.ANY)
    half = jnp.bfloat16
    left_tri, left_diag, grad_diag, proj = pl.pallas_call(
        gram_kernel,
        in_specs=[vmem],
        out_specs=(anywhere, vmem, vmem, anywhere),
        out_shape=(
            jax.ShapeDtypeStruct((TALL, SUB), half),
            jax.ShapeDtypeStruct((1, BLOCK), jnp.float32),
            jax.ShapeDtypeStruct((1, cols_dev), jnp.float32),
            jax.ShapeDtypeStruct((BLOCK, cols_dev), half),
        ),
        scratch_shapes=[
            pltpu.VMEM((TALL, SUB), half),
            pltpu.VMEM((TALL, SUB), half),
            pltpu.VMEM((TALL // 2, SUB), half),
            pltpu.VMEM((TALL // 4, SUB), half),
            pltpu.VMEM((TALL // 8, SUB), half),
            pltpu.VMEM((col_blocks * TALL, SUB), half),
            pltpu.VMEM((col_blocks * TALL, SUB), half),
            pltpu.VMEM((col_blocks * TALL // 2, SUB), half),
            pltpu.VMEM((col_blocks * TALL // 2, SUB), half),
            pltpu.VMEM((4, 1, BLOCK), jnp.float32),
            pltpu.VMEM((3, 1, BLOCK), jnp.float32),
            pltpu.VMEM((3, 1, cols_dev), jnp.float32),
            pltpu.VMEM((2, 1, cols_dev), jnp.float32),
            pltpu.VMEM((BLOCK, BLOCK), half),
            pltpu.VMEM((BLOCK, cols_dev), half),
            pltpu.SemaphoreType.DMA((35,)),
            pltpu.SemaphoreType.DMA((35,)),
            pltpu.SemaphoreType.DMA((5,)),
        ],
        compiler_params=pltpu.CompilerParams(
            vmem_limit_bytes=VMEM_LIMIT, collective_id=0, has_side_effects=True
        ),
    )(gradient)
    return pl.pallas_call(
        apply_kernel,
        grid=(col_blocks,),
        in_specs=[
            pl.BlockSpec((BLOCK, BLOCK), lambda j: (0, j)),
            pl.BlockSpec((1, BLOCK), lambda j: (0, j)),
            pl.BlockSpec((TALL, SUB), lambda j: (0, 0)),
            pl.BlockSpec((1, BLOCK), lambda j: (0, 0)),
        ],
        out_specs=pl.BlockSpec((BLOCK, BLOCK), lambda j: (0, j)),
        out_shape=jax.ShapeDtypeStruct((BLOCK, cols_dev), jnp.bfloat16),
        scratch_shapes=[
            pltpu.VMEM((BLOCK, BLOCK), jnp.bfloat16),
            pltpu.VMEM((BLOCK, BLOCK), jnp.float32),
        ],
        compiler_params=params,
    )(proj, grad_diag, left_tri, left_diag)


def solution(mesh):
    in_specs = (P("row", "col"),)
    out_specs = P("row", "col")
    return jax.shard_map(local, mesh=mesh, in_specs=in_specs, out_specs=out_specs, check_vma=False)
```

time: 145 us -> 150 us (1.034)
  Pallas kernels: 144 us -> 149 us
    pallas_call x1, Pallas kernels: 98.1 us -> 125 us  [local(): pl.pallas_call(gram_kernel, in_specs=[vmem], out_specs=(anywhere, vmem, v...]
    pallas_call x1, Pallas kernels: 45.9 us -> 24.7 us  [local(): pl.pallas_call(apply_kernel, grid=(col_blocks,), in_specs=[pl.BlockSpec((...]
where the time goes in v3:
time: 150 us; the launch traced here: 149 us
  Pallas kernels  149 us (99%)
    pallas_call x1, Pallas kernels, local(): pl.pallas_call(gram_kernel, in_specs=[vmem], out_specs=(anywhere, vmem, v...  125 us
    pallas_call x1, Pallas kernels, local(): pl.pallas_call(apply_kernel, grid=(col_blocks,), in_specs=[pl.BlockSpec((...  24.7 us

profile of v3, /device:TPU:0, one launch (start us, length us, event | category | flops | bytes accessed | tf_op | source)
XLA Modules:
  0.0 149.5 jit_solution(8773347173143163312)
XLA Ops:
  0.0 124.8 %shard_map.17 = (bf16[5376,256]{1,0:T(8,128)(2,1)}, f32[1,1536]{1,0:T(1,128)}, f32[1,3072]{1,0:T(1,128)}, bf16[1536,3072]{1,0:T(8,128)(2,1)}) custom-call(bf16[1536,3072]{1,0:T(8,128)(2,1)} %g_ref.1), custom_call_target="tpu_custom_call" | custom-call | tf_op jit(solution)/shard_map/pallas_call | solution.py:477
  124.8 24.7 %shard_map.18 = bf16[1536,3072]{1,0:T(8,128)(2,1)} custom-call(bf16[1536,3072]{1,0:T(8,128)(2,1)} %get-tuple-element.9.proj_ref, f32[1,3072]{1,0:T(1,128)} %get-tuple-element.10.grad_ref, bf16[5376,256]{1,0:T(8,128)(2,1)} %get-tuple-element.11.left_ref, f32[1,1536]{1,0:T(1,128)} %get-tuple-element.12.left_diag), custom_call_target="tpu_custom_call" | custom-call | tf_op jit(solution)/shard_map/pallas_call | solution.py:511
